TPU v7x, 32 devices: a whole 2x2x4 slice. The times are simulated.
32 devices in a mesh: box: 4 (over z), slab: 8 (over y, x, core).
Axes of the slice: x: 2, y: 2, z: 4, core: 2. Of those that a mesh axis runs over, the one named last changes fastest.
Arguments:
- hidden_field: bfloat16 [4, 8, 64, 128, 128], P('box', None, 'slab'), may hold values from -6 to 6
- cone_grad: float32 [256, 128, 128], P(('box', 'slab')), may hold values from -6 to 6
- conv_weight: bfloat16 [8, 27], replicated, may hold values from -0.4375 to 0.4375
- box_lower: int32 [256], P(('box', 'slab')), may hold values from 0 to 3, as said below
- box_upper: int32 [256], P(('box', 'slab')), may hold values from 0 to 3, as said below
- plane_lower: int32 [256], P(('box', 'slab')), may hold values from 0 to 63, as said below
- plane_upper: int32 [256], P(('box', 'slab')), may hold values from 0 to 63, as said below
- weight_lower: int32 [256], P(('box', 'slab')), may hold values from 0 to 256
- weight_upper: int32 [256], P(('box', 'slab')), may hold values from 0 to 256, as said below
Outputs:
- hidden_grad: bfloat16 [4, 8, 64, 128, 128], P('box', None, 'slab')
- weight_grad: float32 [8, 27], replicated
Inputs may be any that keep to these rules, and one draw needn't show every extreme that they name: With g = l // 64 the group of plane l, box_lower[l] is g or g - 1 (never below 0). box_upper[l] = min(box_lower[l] + 1, 3). Each box b has one offset o_b, and for one box, drawn from the seed, o_b = 32; plane_lower[l] = (l + o_b) mod 64 with b = box_lower[l]. plane_upper[l] = (l + o_b) mod 64 with b = box_upper[l], the same offsets. weight_upper[l] = 256 - weight_lower[l].
All inputs are finite; a program needn't handle non-finite values.
Results may differ from a plain program's by a relative error of at most 0.005.
Values may be sent and summed in bfloat16 or wider, within the bound.
A program may use at most 320 MiB of HBM per device.

v0:
```python
import math

import jax
import jax.numpy as jnp
from jax import lax
from jax.sharding import PartitionSpec as P

WDEN = 256


def passed_along(value, axis, steps):
    count = lax.axis_size(axis)
    first, last = (max(0, -steps), min(count, count - steps))
    return lax.ppermute(value, axis, [(source, source + steps) for source in range(first, last)])


def with_halo(cells, sides, width):
    for axis, dim in sides:
        count = lax.axis_size(axis)
        head = lax.slice_in_dim(cells, 0, width, axis=dim)
        tail = lax.slice_in_dim(cells, cells.shape[dim] - width, cells.shape[dim], axis=dim)
        cells = jnp.concatenate(
            [
                lax.ppermute(tail, axis, [(i, (i + 1) % count) for i in range(count)]),
                cells,
                lax.ppermute(head, axis, [((i + 1) % count, i) for i in range(count)]),
            ],
            axis=dim,
        )
    return cells


def wrap_sides(field):
    field = jnp.concatenate([field[:, -1:], field, field[:, :1]], 1)
    return jnp.concatenate([field[:, :, -1:], field, field[:, :, :1]], 2)


def local(
    hidden_field,
    cone_grad,
    conv_weight,
    box_lower,
    box_upper,
    plane_lower,
    plane_upper,
    weight_lower,
    weight_upper,
):
    group = lax.axis_index("box")
    column = lax.axis_index("slab")
    slab_count = lax.axis_size("slab")
    depth = cone_grad.shape[0]
    total_planes = depth * slab_count
    lower = weight_lower.astype(jnp.float32) / WDEN
    upper = weight_upper.astype(jnp.float32) / WDEN
    own_coef = jnp.where(box_lower == group, lower, 0.0) + jnp.where(box_upper == group, upper, 0.0)
    below_coef = jnp.where(box_lower == group - 1, lower, 0.0)
    above_coef = jnp.where(box_upper == group + 1, upper, 0.0)
    for_below = below_coef[:, None, None] * cone_grad
    for_above = above_coef[:, None, None] * cone_grad
    from_above = passed_along(for_below, "box", -1)
    from_below = passed_along(for_above, "box", 1)
    merged = (own_coef[:, None, None] * cone_grad + from_above + from_below).astype(jnp.bfloat16)
    first_plane = jnp.where(box_lower[0] == group, plane_lower[0], plane_upper[0])
    offset = (first_plane - column * depth) % total_planes
    whole = lax.all_gather(merged, "slab", axis=0, tiled=True)
    wanted = (column * depth + jnp.arange(depth, dtype=jnp.int32) - offset) % total_planes
    field_low = jnp.take(whole, wanted, axis=0)
    padded = with_halo(field_low, (("slab", 0),), 1)
    padded = wrap_sides(padded)[None, None]
    channel_count = hidden_field.shape[1]
    kernel = conv_weight.reshape(channel_count, 1, 3, 3, 3)[:, :, ::-1, ::-1, ::-1]
    numbers = ("NCDHW", "OIDHW", "NCDHW")
    hidden_grad = lax.conv_general_dilated(
        padded,
        kernel,
        (1, 1, 1),
        "VALID",
        dimension_numbers=numbers,
        preferred_element_type=jnp.float32,
    )
    hidden_grad = hidden_grad.astype(jnp.bfloat16).reshape(hidden_field.shape)
    as_kernel = hidden_field.reshape(
        channel_count, 1, depth, hidden_field.shape[3], hidden_field.shape[4]
    )
    partial_value = lax.conv_general_dilated(
        padded,
        as_kernel,
        (1, 1, 1),
        "VALID",
        dimension_numbers=numbers,
        preferred_element_type=jnp.float32,
    )
    partial_value = partial_value[0][:, ::-1, ::-1, ::-1].reshape(channel_count, 27)
    total = lax.psum(partial_value, ("box", "slab"))
    cells = lax.axis_size("box") * total_planes * field_low.shape[1] * field_low.shape[2]
    weight_grad = total * (1.0 / math.sqrt(cells))
    return (hidden_grad, weight_grad)


def solution(mesh):
    in_specs = (
        P("box", None, "slab", None, None),
        P(("box", "slab"), None, None),
        P(),
        P(("box", "slab")),
        P(("box", "slab")),
        P(("box", "slab")),
        P(("box", "slab")),
        P(("box", "slab")),
        P(("box", "slab")),
    )
    out_specs = (P("box", None, "slab", None, None), P())
    return jax.shard_map(local, mesh=mesh, in_specs=in_specs, out_specs=out_specs, check_vma=False)
```

profile of v0, /device:TPU:0, one launch (start us, length us, event | category | flops | bytes accessed | tf_op | source)
XLA Modules:
  0.0 805.5 jit_solution(18228177344446519526)
XLA Ops:
  7.2 0.0 all-gather.2.cloned.1.call-start
  7.2 0.7 fusion.3
  8.0 1.2 broadcast_multiply_fusion.1
  9.1 0.0 copy-start.6
  9.2 1.4 collective-permute-start
  10.6 5.6 collective-permute-start.1
  16.2 10.0 %collective-permute-done = f32[8,128,128]{2,1,0:T(8,128)S(1)} collective-permute-done((f32[8,128,128]{2,1,0:T(8,128)S(1)}, f32[8,128,128]{2,1,0:T(8,128)S(1)}, u32[]{:S(2)}, u32[]{:S(2)}) %collective-permute-start) | collective-permute-done | bytes 524320 | tf_op jit(solution)/shard_map/ppermute | solution.py:14
  26.1 1.2 collective-permute-done.1
  27.3 1.9 add_convert_fusion
  29.2 0.0 all-gather.2.cloned.1.call-update
  29.2 0.0 copy-done.16
  29.4 30.2 %all-gather.2.cloned.1.call-done = bf16[64,128,128]{2,1,0:T(8,128)(2,1)} async-done(((bf16[8,128,128]{2,1,0:T(8,128)(2,1)}), bf16[64,128,128]{2,1,0:T(8,128)(2,1)}) %all-gather.2.cloned.1.call-update) | async-done | bytes 2097168 | tf_op jit(solution)/shard_map/all_gather | solution.py:66
  59.6 2.2 gather_fusion
  61.8 0.1 broadcast_select_fusion
  61.9 0.3 collective-permute-start.2
  62.3 2.4 collective-permute-start.3
  64.6 69.5 %copy.41 = bf16[8,1,8,128,128]{0,1,4,3,2:T(2,128)(2,1)} copy(bf16[8,1,8,128,128]{4,3,2,0,1:T(8,128)(2,1)S(1)} %bitcast.34) | data formatting | bytes 4194304 | tf_op jit(solution)/shard_map/reshape | solution.py:83
  134.1 0.0 copy-done.14
  134.1 0.1 copy.36
  134.2 0.6 reshape.96
  134.9 0.0 collective-permute-done.2
  134.9 0.0 collective-permute-done.3
  134.9 0.1 pad_maximum_fusion.1
  135.0 0.2 fusion.7
  135.2 0.0 copy-start.4
  135.2 0.7 copy-done.2
  135.9 0.1 copy-done.4
  136.0 0.6 fusion.15
  136.6 0.0 copy-done.7
  136.6 0.0 copy-done.9
  136.6 184.9 %copy.40 = bf16[1,1,10,130,130]{1,0,4,3,2:T(2,128)(2,1)} copy(bf16[1,1,10,130,130]{4,3,2,1,0:T(8,128)(2,1)S(1)} %fusion.15) | data formatting | bytes 676000 | tf_op jit(solution)/shard_map/broadcast_in_dim | solution.py:70
  321.5 0.0 copy-done.11
  321.6 0.0 copy-start.5
  321.6 0.0 copy-start.8
  321.6 253.9 %fusion.9 = f32[1,8,3,3,3]{1,0,4,3,2:T(1,128)S(1)} fusion(bf16[1,1,10,130,130]{1,0,4,3,2:T(2,128)(2,1)} %copy.40, bf16[8,1,8,128,128]{0,1,4,3,2:T(2,128)(2,1)} %copy.41), kind=kOutput, calls=%fused_computation.40 | convolution fusion | flops 56623104 | bytes 2436016 | tf_op jit(solution)/shard_map/conv_general_dilated | solution.py:86
  575.5 39.6 %psum.7 = f32[8,27]{0,1:T(8,128)S(1)} all-reduce(f32[8,27]{0,1:T(8,128)S(1)} %reshape.75), channel_id=1, replica_groups=mesh['box'=4,'slab'=8] {'box','slab'}, use_global_device_ids=true, to_apply=%region_0.1 | all-reduce | flops 216 | bytes 1728 | tf_op jit(solution)/shard_map/psum | solution.py:95
  615.2 0.7 copy.43
  615.9 1.3 fusion.16
  617.1 0.4 copy.47
  617.5 0.1 pad.clone
  617.6 0.3 reshape.78
  618.0 0.4 fusion.2
  618.3 33.7 %copy.37 = bf16[1,10,130,8,19]{3,0,4,2,1:T(2,128)(2,1)} copy(bf16[1,10,130,8,19]{2,4,3,1,0:T(8,128)(2,1)S(1)} %fusion.2) | data formatting | bytes 790400 | tf_op jit(solution)/shard_map/conv_general_dilated | solution.py:74
  652.0 112.6 %fusion.10 = bf16[8,128,8,17,8]{4,2,3,1,0:T(8,128)(2,1)} fusion(bf16[1,10,130,8,19]{3,0,4,2,1:T(2,128)(2,1)} %copy.37, bf16[8,1,3,3,3]{0,1,4,3,2:T(2,128)(2,1)S(1)} %copy-done.13), kind=kOutput, calls=%fused_computation.41 | convolution fusion | flops 60162048 | bytes 2623856 | tf_op jit(solution)/shard_map/conv_general_dilated | solution.py:74
  764.6 30.5 %copy.39 = bf16[8,128,8,17,8]{1,4,3,2,0:T(8,128)(2,1)S(1)} copy(bf16[8,128,8,17,8]{4,2,3,1,0:T(8,128)(2,1)} %fusion.10) | data formatting | bytes 4456448 | tf_op jit(solution)/shard_map/conv_general_dilated | solution.py:74
  795.1 0.5 select_convert_fusion
  795.7 0.1 slice_bitcast_fusion
  795.8 2.9 copy.42
  (37 shorter events, 0.2 us)
Async XLA Ops:
  7.2 22.1 %copy-start.16 = (s32[8]{0:T(128)S(1)}, s32[8]{0:T(128)}, u32[]{:S(2)}) copy-start(s32[8]{0:T(128)} %param.12) | copy-start | bytes 100
  7.2 22.1 %copy-start.17 = (s32[8]{0:T(128)S(1)}, s32[8]{0:T(128)}, u32[]{:S(2)}) copy-start(s32[8]{0:T(128)} %param.14) | copy-start | bytes 100
  7.2 22.1 %copy-start.18 = (s32[8]{0:T(128)S(1)}, s32[8]{0:T(128)}, u32[]{:S(2)}) copy-start(s32[8]{0:T(128)} %param.15) | copy-start | bytes 100
  7.2 52.4 %all-gather.2.cloned.1.call-start = ((), (), s32[]{:S(2)}) async-start(), calls=%async_computation | async-start | bytes 2359296 | tf_op jit(solution)/shard_map/all_gather | solution.py:66
  9.1 55.5 %copy-start.6 = (bf16[1,8,8,128,128]{4,3,2,1,0:T(8,128)(2,1)S(1)}, bf16[1,8,8,128,128]{4,3,2,1,0:T(8,128)(2,1)}, u32[]{:S(2)}) copy-start(bf16[1,8,8,128,128]{4,3,2,1,0:T(8,128)(2,1)} %param.9) | copy-start | bytes 6291460
  9.2 17.0 %collective-permute-start = (f32[8,128,128]{2,1,0:T(8,128)S(1)}, f32[8,128,128]{2,1,0:T(8,128)S(1)}, u32[]{:S(2)}, u32[]{:S(2)}) collective-permute-start(f32[8,128,128]{2,1,0:T(8,128)S(1)} %get-tuple-element.8), channel_id=1, source_target_pairs={{8,0},{16,8},{24,16},{9,1},{17,9},{25,17},{10,2},{18,10},{26,18},{... | collective-permute-start | bytes 1572872 | tf_op jit(solution)/shard_map/ppermute | solution.py:14
  10.6 16.7 %collective-permute-start.1 = (f32[8,128,128]{2,1,0:T(8,128)S(1)}, f32[8,128,128]{2,1,0:T(8,128)S(1)}, u32[]{:S(2)}, u32[]{:S(2)}) collective-permute-start(f32[8,128,128]{2,1,0:T(8,128)S(1)} %get-tuple-element.9), channel_id=1, source_target_pairs={{0,8},{8,16},{16,24},{1,9},{9,17},{17,25},{2,10},{10,18},{18,26},{... | collective-permute-start | bytes 1572872 | tf_op jit(solution)/shard_map/ppermute | solution.py:14
  61.9 73.3 %copy-start = (bf16[8,128,128]{2,1,0:T(8,128)(2,1)}, bf16[8,128,128]{2,1,0:T(8,128)(2,1)S(1)}, u32[]{:S(2)}) copy-start(bf16[8,128,128]{2,1,0:T(8,128)(2,1)S(1)} %broadcast_select_fusion) | copy-start | bytes 786436
  61.9 72.9 %collective-permute-start.2 = (bf16[1,128,128]{2,1,0:T(8,128)(2,1)S(1)}, bf16[1,128,128]{2,1,0:T(8,128)(2,1)S(1)}, u32[]{:S(2)}, u32[]{:S(2)}) collective-permute-start(bf16[1,128,128]{2,1,0:T(8,128)(2,1)S(1)} %get-tuple-element.14), channel_id=1, source_target_pairs={{0,1},{1,2},{2,3},{3,4},{4,5},{5,6},{6,7},{7,0},{8,9},{9,10},{10,1... | collective-permute-start | bytes 98312 | tf_op jit(solution)/shard_map/ppermute | solution.py:24
  62.3 72.6 %collective-permute-start.3 = (bf16[1,128,128]{2,1,0:T(8,128)(2,1)S(1)}, bf16[1,128,128]{2,1,0:T(8,128)(2,1)S(1)}, u32[]{:S(2)}, u32[]{:S(2)}) collective-permute-start(bf16[1,128,128]{2,1,0:T(8,128)(2,1)S(1)} %get-tuple-element.15), channel_id=1, source_target_pairs={{1,0},{2,1},{3,2},{4,3},{5,4},{6,5},{7,6},{0,7},{9,8},{10,9},{11,1... | collective-permute-start | bytes 98312 | tf_op jit(solution)/shard_map/ppermute | solution.py:26
  64.6 69.5 %copy-start.14 = (bf16[8,27]{1,0:T(8,128)(2,1)S(1)}, bf16[8,27]{1,0:T(8,128)(2,1)}, u32[]{:S(2)}) copy-start(bf16[8,27]{1,0:T(8,128)(2,1)} %param.11) | copy-start | bytes 1300
  134.9 1.8 copy-start.7
  134.9 1.8 copy-start.9
  134.9 186.7 %copy-start.11 = (bf16[10,1,128]{2,1,0:T(2,128)(2,1)}, bf16[10,1,128]{2,1,0:T(2,128)(2,1)S(1)}, u32[]{:S(2)}) copy-start(bf16[10,1,128]{2,1,0:T(2,128)(2,1)S(1)} %get-tuple-element.12) | copy-start | bytes 7684
  134.9 186.6 %copy-start.12 = (bf16[10,1,128]{2,1,0:T(2,128)(2,1)}, bf16[10,1,128]{2,1,0:T(2,128)(2,1)S(1)}, u32[]{:S(2)}) copy-start(bf16[10,1,128]{2,1,0:T(2,128)(2,1)S(1)} %get-tuple-element.13) | copy-start | bytes 7684
  135.2 0.7 copy-start.2
  135.2 0.8 copy-start.4
  321.6 294.3 %copy-start.1 = (bf16[8,128,128]{2,1,0:T(8,128)(2,1)S(1)}, bf16[8,128,128]{2,1,0:T(8,128)(2,1)}, u32[]{:S(2)}) copy-start(bf16[8,128,128]{2,1,0:T(8,128)(2,1)} %copy-done) | copy-start | bytes 786436
  321.6 294.3 %copy-start.3 = (bf16[10,130,1]{2,1,0:T(8,128)(2,1)S(1)}, bf16[10,130,1]{2,1,0:T(8,128)(2,1)}, u32[]{:S(2)}) copy-start(bf16[10,130,1]{2,1,0:T(8,128)(2,1)} %copy-done.2) | copy-start | bytes 7804
  321.6 294.3 %copy-start.5 = (bf16[10,130,1]{2,1,0:T(8,128)(2,1)S(1)}, bf16[10,130,1]{2,1,0:T(8,128)(2,1)}, u32[]{:S(2)}) copy-start(bf16[10,130,1]{2,1,0:T(8,128)(2,1)} %copy-done.4) | copy-start | bytes 7804
  321.6 294.3 %copy-start.8 = (bf16[1,128,128]{2,1,0:T(8,128)(2,1)S(1)}, bf16[1,128,128]{2,1,0:T(8,128)(2,1)}, u32[]{:S(2)}) copy-start(bf16[1,128,128]{2,1,0:T(8,128)(2,1)} %copy-done.7) | copy-start | bytes 98308
  321.6 294.3 %copy-start.10 = (bf16[1,128,128]{2,1,0:T(8,128)(2,1)S(1)}, bf16[1,128,128]{2,1,0:T(8,128)(2,1)}, u32[]{:S(2)}) copy-start(bf16[1,128,128]{2,1,0:T(8,128)(2,1)} %copy-done.9) | copy-start | bytes 98308
  618.3 33.7 %copy-start.13 = (bf16[8,1,3,3,3]{0,1,4,3,2:T(2,128)(2,1)S(1)}, bf16[8,1,3,3,3]{0,1,4,3,2:T(2,128)(2,1)}, u32[]{:S(2)}) copy-start(bf16[8,1,3,3,3]{0,1,4,3,2:T(2,128)(2,1)} %reshape.96) | copy-start | bytes 1300
  764.6 30.5 %copy-start.15 = (pred[8,17]{1,0:T(8,128)(4,1)S(1)}, pred[8,17]{1,0:T(8,128)(4,1)}, u32[]{:S(2)}) copy-start(pred[8,17]{1,0:T(8,128)(4,1)} %constant.70) | copy-start | bytes 412
Sparse Core Ops, SparseCore 0:
  29.3 30.2 all-gather.1
where the time goes:
time: 806 us
  matrix products  366 us (45%)
  local copies, waits for them, and re-layouts  327 us (41%)
  waiting for transfers between devices  41.4 us (5%)
  blocking collectives  39.6 us (5%)
  between operations  14.5 us (2%)
  starting transfers between devices  9.75 us (1%)
    conv_general_dilated x1, matrix products, local(): lax.conv_general_dilated(padded, as_kernel, (1, 1, 1), 'VALID', dimension...  254 us
    broadcast_in_dim x2, local copies, waits for them, and re-layouts, local(): padded = wrap_sides(padded)[None, None]  185 us
    conv_general_dilated x1, matrix products, local(): lax.conv_general_dilated(padded, kernel, (1, 1, 1), 'VALID', dimension_nu...  113 us
    reshape x1, local copies, waits for them, and re-layouts, local(): hidden_field.reshape(channel_count, 1, depth, hidden_field.shape[3], hidd...  69.5 us
    conv_general_dilated x4, local copies, waits for them, and re-layouts, local(): lax.conv_general_dilated(padded, kernel, (1, 1, 1), 'VALID', dimension_nu...  64.5 us
    psum x1, blocking collectives, local(): total = lax.psum(partial_value, ('box', 'slab'))  39.6 us
    all_gather x1, waiting for transfers between devices, local(): whole = lax.all_gather(merged, 'slab', axis=0, tiled=True)  30.2 us
  transfers between devices with their start and end apart: 5, of which 3 were waited for; matrix products, arithmetic and copies ran while one was open for 9% of the time, Pallas kernels for 0%

commit v1 on v0

v1 whole, which is shorter than its diff:
```python
import functools
import math

import jax
import jax.numpy as jnp
from jax import lax
from jax.experimental import pallas as pl
from jax.experimental.pallas import tpu as pltpu
from jax.sharding import PartitionSpec as P

WDEN = 256
MESH = pl.DeviceIdType.MESH
F32 = jnp.float32
BF16 = jnp.bfloat16
TAP_ROWS = 32


def kernel(
    nbox,
    nslab,
    scale,
    bl,
    bu,
    plo,
    pup,
    wl,
    wu,
    cone,
    weight,
    h_hbm,
    out_hbm,
    wg,
    hbuf,
    own,
    z_up,
    z_dn,
    from_above,
    from_below,
    send_a,
    recv_a,
    send_b,
    recv_b,
    ht,
    wmat,
    wide,
    lmat,
    part,
    obuf,
    msg,
    slab_terms,
    msg2,
    box_terms,
    hsem,
    up_s,
    up_r,
    dn_s,
    dn_r,
    a_s,
    a_r,
    b_s,
    b_r,
    c_s,
    c_r,
    d_s,
    d_r,
    osem,
):
    g = lax.axis_index("box")
    me = lax.axis_index("slab")
    depth, nx, ny = cone.shape
    rows = nx // nslab
    nz = depth * nslab
    ch = hbuf.shape[0]
    pairs = ch // 2

    h_copy = pltpu.make_async_copy(h_hbm, hbuf, hsem)
    h_copy.start()

    barrier = pltpu.get_barrier_semaphore()

    def greet_slab(j, _):
        pl.semaphore_signal(barrier, inc=1, device_id={"slab": lax.rem(me + j, nslab)}, device_id_type=MESH)
        return 0

    def greet_box(j, _):
        pl.semaphore_signal(barrier, inc=1, device_id={"box": lax.rem(g + j, nbox)}, device_id_type=MESH)
        return 0

    lax.fori_loop(1, nslab, greet_slab, 0)
    lax.fori_loop(1, nbox, greet_box, 0)

    def weigh(i, _):
        lower = wl[i].astype(F32) * (1.0 / WDEN)
        upper = wu[i].astype(F32) * (1.0 / WDEN)
        own_c = jnp.where(bl[i] == g, lower, 0.0) + jnp.where(bu[i] == g, upper, 0.0)
        below_c = jnp.where(bl[i] == g - 1, lower, 0.0)
        above_c = jnp.where(bu[i] == g + 1, upper, 0.0)
        plane = cone[i].reshape(nslab, rows, ny)
        z_up[:, i] = (above_c * plane).astype(z_up.dtype)
        z_dn[:, i] = (below_c * plane).astype(z_dn.dtype)
        own[:, i] = own_c * plane
        return 0

    lax.fori_loop(0, depth, weigh, 0)
    pl.semaphore_wait(barrier, nslab - 1 + nbox - 1)

    def up_copy(t):
        return pltpu.make_async_remote_copy(
            src_ref=z_up.at[t],
            dst_ref=from_below.at[t],
            send_sem=up_s.at[t],
            recv_sem=up_r.at[t],
            device_id={"box": lax.rem(g + 1, nbox)},
            device_id_type=MESH,
        )

    def dn_copy(t):
        return pltpu.make_async_remote_copy(
            src_ref=z_dn.at[t],
            dst_ref=from_above.at[t],
            send_sem=dn_s.at[t],
            recv_sem=dn_r.at[t],
            device_id={"box": lax.rem(g + nbox - 1, nbox)},
            device_id_type=MESH,
        )

    def send_z(j, _):
        t = lax.rem(me + 1 + j, nslab)

        @pl.when(g < nbox - 1)
        def _():
            up_copy(t).start()

        @pl.when(g > 0)
        def _():
            dn_copy(t).start()

        return 0

    lax.fori_loop(0, nslab, send_z, 0)

    h_copy.wait()

    def turn(c, _):
        for z in range(depth):
            ht[pl.ds(pl.multiple_of(c * ny, ny), ny), z * nx : (z + 1) * nx] = hbuf[c, z].T
        return 0

    lax.fori_loop(0, ch, turn, 0)

    def merge(t):
        @pl.when(g < nbox - 1)
        def _():
            dn_copy(t).wait_recv()
            own[t] = own[t] + from_above[t].astype(F32)

        @pl.when(g > 0)
        def _():
            up_copy(t).wait_recv()
            own[t] = own[t] + from_below[t].astype(F32)

    def a_copy(t, source):
        return pltpu.make_async_remote_copy(
            src_ref=send_a.at[t],
            dst_ref=recv_a.at[pl.ds(source * depth, depth)],
            send_sem=a_s.at[t],
            recv_sem=a_r.at[source],
            device_id={"slab": t},
            device_id_type=MESH,
        )

    def merge_send(j, _):
        t = lax.rem(me + 1 + j, nslab)
        merge(t)
        send_a[t] = own[t].astype(BF16)
        a_copy(t, me).start()
        return 0

    lax.fori_loop(0, nslab - 1, merge_send, 0)
    merge(me)
    recv_a[pl.ds(me * depth, depth)] = own[me].astype(BF16)

    y_in = lax.broadcasted_iota(jnp.int32, (ny, ny), 0)
    y_out = lax.broadcasted_iota(jnp.int32, (ny, ny), 1)
    hits = [y_in == lax.rem(y_out - dy + ny, ny) for dy in (-1, 0, 1)]
    taps = weight[...].astype(F32)
    for k in range(27):
        wide[k] = jnp.broadcast_to(taps[:, k : k + 1], (ch, ny))

    def fill(p, _):
        for cc in range(2):
            for j in range(9):
                block = jnp.zeros((ny, ny), F32)
                for d in range(3):
                    block = jnp.where(hits[d], wide[3 * j + d, pl.ds(2 * p + cc, 1)], block)
                wmat[p, j * ny : (j + 1) * ny, cc * ny : (cc + 1) * ny] = block.astype(BF16)
        return 0

    lax.fori_loop(0, pairs, fill, 0)

    def wait_a(j, _):
        source = lax.rem(me + j, nslab)
        a_copy(source, source).wait_recv()
        return 0

    lax.fori_loop(1, nslab, wait_a, 0)

    offset = jnp.where(bl[0] == g, plo[0], pup[0]) - me * depth

    def wanted(s, q):
        return recv_a[lax.rem(s * depth - 1 + q - offset + 2 * nz, nz)]

    def b_copy(s, source):
        return pltpu.make_async_remote_copy(
            src_ref=send_b.at[s],
            dst_ref=recv_b.at[source],
            send_sem=b_s.at[s],
            recv_sem=b_r.at[source],
            device_id={"slab": s},
            device_id_type=MESH,
        )

    def turn_send(j, _):
        s = lax.rem(me + 1 + j, nslab)
        for q in range(depth + 2):
            send_b[s, q] = wanted(s, q)
        b_copy(s, me).start()
        return 0

    lax.fori_loop(0, nslab - 1, turn_send, 0)
    for q in range(depth + 2):
        recv_b[me, q] = wanted(me, q)

    def wait_b(j, _):
        source = lax.rem(me + j, nslab)
        b_copy(source, source).wait_recv()
        return 0

    lax.fori_loop(1, nslab, wait_b, 0)

    for q in range(depth + 2):
        plane = recv_b[:, q].astype(F32).reshape(nx, ny)
        for dx in (-1, 0, 1):
            moved = (plane if dx == 0 else pltpu.roll(plane, dx % nx, 0)).astype(BF16)
            for dz in (-1, 0, 1):
                z, j = q + dz - 1, (dz + 1) * 3 + dx + 1
                if 0 <= z < depth:
                    lmat[z * nx : (z + 1) * nx, j * ny : (j + 1) * ny] = moved

    part[...] = jnp.zeros_like(part)
    picks = [y_out == lax.rem(y_in - dy + ny, ny) for dy in (-1, 0, 1)]

    def pair_terms(p, _):
        prod = jnp.dot(
            ht[pl.ds(pl.multiple_of(p * 2 * ny, 2 * ny), 2 * ny), :], lmat[...], preferred_element_type=F32
        )
        for cc in range(2):
            for j in range(9):
                block = prod[cc * ny : (cc + 1) * ny, j * ny : (j + 1) * ny]
                for d in range(3):
                    row = cc * TAP_ROWS + 3 * j + d
                    part[p, row : row + 1] = jnp.sum(jnp.where(picks[d], block, 0.0), axis=0, keepdims=True)
        return 0

    lax.fori_loop(0, pairs, pair_terms, 0)
    msg[...] = jnp.zeros_like(msg)
    for half in range(pairs // 2):
        both = part[2 * half : 2 * half + 2].reshape(4 * TAP_ROWS, ny)
        msg[half : half + 1] = jnp.sum(both.T, axis=0, keepdims=True)

    def c_copy(s, source):
        return pltpu.make_async_remote_copy(
            src_ref=msg,
            dst_ref=slab_terms.at[source],
            send_sem=c_s.at[s],
            recv_sem=c_r.at[source],
            device_id={"slab": s},
            device_id_type=MESH,
        )

    def d_copy(b, source):
        return pltpu.make_async_remote_copy(
            src_ref=msg2,
            dst_ref=box_terms.at[source],
            send_sem=d_s.at[b],
            recv_sem=d_r.at[source],
            device_id={"box": b},
            device_id_type=MESH,
        )

    def send_c(j, _):
        c_copy(lax.rem(me + j, nslab), me).start()
        return 0

    def send_d(j, _):
        d_copy(lax.rem(g + j, nbox), g).start()
        return 0

    def wait_c(j, _):
        source = lax.rem(me + j, nslab)
        c_copy(source, source).wait_recv()
        return 0

    def wait_d(j, _):
        source = lax.rem(g + j, nbox)
        d_copy(source, source).wait_recv()
        return 0

    def o_copy(p):
        return pltpu.make_async_copy(obuf.at[pl.ds(2 * p, 2)], out_hbm.at[pl.ds(2 * p, 2)], osem.at[p])

    def pair_grads(p, _):
        grads = jnp.dot(lmat[...], wmat[p], preferred_element_type=F32)
        for cc in range(2):
            obuf[2 * p + cc] = grads[:, cc * ny : (cc + 1) * ny].reshape(depth, nx, ny).astype(BF16)
        o_copy(p).start()
        return 0

    slab_terms[me] = msg[...]
    lax.fori_loop(1, nslab, send_c, 0)
    lax.fori_loop(0, pairs // 2, pair_grads, 0)
    lax.fori_loop(1, nslab, wait_c, 0)
    total = slab_terms[0]
    for s in range(1, nslab):
        total = total + slab_terms[s]
    msg2[...] = total
    box_terms[g] = total
    lax.fori_loop(1, nbox, send_d, 0)
    lax.fori_loop(pairs // 2, pairs, pair_grads, 0)
    lax.fori_loop(1, nbox, wait_d, 0)
    total = box_terms[0]
    for b in range(1, nbox):
        total = total + box_terms[b]
    total = total * scale
    for c in range(ch):
        at = (c % 4) * TAP_ROWS
        wg[c : c + 1, :] = total[c // 4 : c // 4 + 1, at : at + 27]

    def drain_z(t, _):
        @pl.when(g < nbox - 1)
        def _():
            up_copy(t).wait_send()

        @pl.when(g > 0)
        def _():
            dn_copy(t).wait_send()

        return 0

    def drain_slab(j, _):
        s = lax.rem(me + j, nslab)
        a_copy(s, me).wait_send()
        b_copy(s, me).wait_send()
        c_copy(s, me).wait_send()
        return 0

    def drain_box(j, _):
        d_copy(lax.rem(g + j, nbox), g).wait_send()
        return 0

    def drain_out(p, _):
        o_copy(p).wait()
        return 0

    lax.fori_loop(0, nslab, drain_z, 0)
    lax.fori_loop(1, nslab, drain_slab, 0)
    lax.fori_loop(1, nbox, drain_box, 0)
    lax.fori_loop(0, pairs, drain_out, 0)


def local(
    nbox,
    nslab,
    hidden_field,
    cone_grad,
    conv_weight,
    box_lower,
    box_upper,
    plane_lower,
    plane_upper,
    weight_lower,
    weight_upper,
):
    _, ch, depth, nx, ny = hidden_field.shape
    rows = nx // nslab
    nz = depth * nslab
    scale = 1.0 / math.sqrt(nbox * nz * nx * ny)
    vmem = pl.BlockSpec(memory_space=pltpu.VMEM)
    smem = pl.BlockSpec(memory_space=pltpu.SMEM)
    anywhere = pl.BlockSpec(memory_space=pl.ANY)
    dma = pltpu.SemaphoreType.DMA
    link = BF16
    hidden_grad, weight_grad = pl.pallas_call(
        functools.partial(kernel, nbox, nslab, scale),
        out_shape=(
            jax.ShapeDtypeStruct((ch, depth, nx, ny), BF16),
            jax.ShapeDtypeStruct((ch, 27), F32),
        ),
        in_specs=[smem] * 6 + [vmem, vmem, anywhere],
        out_specs=(anywhere, vmem),
        scratch_shapes=[
            pltpu.VMEM((ch, depth, nx, ny), BF16),
            pltpu.VMEM((nslab, depth, rows, ny), F32),
            pltpu.VMEM((nslab, depth, rows, ny), link),
            pltpu.VMEM((nslab, depth, rows, ny), link),
            pltpu.VMEM((nslab, depth, rows, ny), link),
            pltpu.VMEM((nslab, depth, rows, ny), link),
            pltpu.VMEM((nslab, depth, rows, ny), BF16),
            pltpu.VMEM((nz, rows, ny), BF16),
            pltpu.VMEM((nslab, depth + 2, rows, ny), BF16),
            pltpu.VMEM((nslab, depth + 2, rows, ny), BF16),
            pltpu.VMEM((ch * ny, depth * nx), BF16),
            pltpu.VMEM((ch // 2, 9 * ny, 2 * ny), BF16),
            pltpu.VMEM((27, ch, ny), F32),
            pltpu.VMEM((depth * nx, 9 * ny), BF16),
            pltpu.VMEM((ch // 2, 2 * TAP_ROWS, ny), F32),
            pltpu.VMEM((ch, depth, nx, ny), BF16),
            pltpu.VMEM((8, 128), F32),
            pltpu.VMEM((nslab, 8, 128), F32),
            pltpu.VMEM((8, 128), F32),
            pltpu.VMEM((nbox, 8, 128), F32),
            dma,
            dma((nslab,)),
            dma((nslab,)),
            dma((nslab,)),
            dma((nslab,)),
            dma((nslab,)),
            dma((nslab,)),
            dma((nslab,)),
            dma((nslab,)),
            dma((nslab,)),
            dma((nslab,)),
            dma((nbox,)),
            dma((nbox,)),
            dma((ch // 2,)),
        ],
        compiler_params=pltpu.CompilerParams(
            collective_id=0, has_side_effects=True, vmem_limit_bytes=44 * 2**20
        ),
    )(
        box_lower,
        box_upper,
        plane_lower,
        plane_upper,
        weight_lower,
        weight_upper,
        cone_grad,
        conv_weight,
        hidden_field.reshape(ch, depth, nx, ny),
    )
    return hidden_grad.reshape(hidden_field.shape), weight_grad


def solution(mesh):
    in_specs = (
        P("box", None, "slab", None, None),
        P(("box", "slab"), None, None),
        P(),
        P(("box", "slab")),
        P(("box", "slab")),
        P(("box", "slab")),
        P(("box", "slab")),
        P(("box", "slab")),
        P(("box", "slab")),
    )
    out_specs = (P("box", None, "slab", None, None), P())
    return jax.shard_map(
        functools.partial(local, mesh.shape["box"], mesh.shape["slab"]),
        mesh=mesh,
        in_specs=in_specs,
        out_specs=out_specs,
        check_vma=False,
    )
```

time: 806 us -> 42.7 us (0.05)
  matrix products: 366 us -> 0 us
  local copies, waits for them, and re-layouts: 327 us -> 9.15 us
  waiting for transfers between devices: 41.4 us -> 0 us
  blocking collectives: 39.6 us -> 0 us
  Pallas kernels: 0 us -> 32.6 us
  between operations: 14.5 us -> 0.66 us
  starting transfers between devices: 9.75 us -> 0 us
    conv_general_dilated x2 -> x0, matrix products: 366 us -> none  [the longest x1 254 us: local(): lax.conv_general_dilated(padded, as_kernel, (1, 1, 1), 'VALID', dimension...]
    broadcast_in_dim x2 -> x0, local copies, waits for them, and re-layouts: 185 us -> none  [local(): padded = wrap_sides(padded)[None, None]]
    reshape x3 -> x0, local copies, waits for them, and re-layouts: 70.1 us -> none  [the longest x1 69.5 us: local(): hidden_field.reshape(channel_count, 1, depth, hidden_field.shape[3], hidd...]
    conv_general_dilated x4 -> x0, local copies, waits for them, and re-layouts: 64.5 us -> none  [local(): lax.conv_general_dilated(padded, kernel, (1, 1, 1), 'VALID', dimension_nu...]
    psum x1 -> x0, blocking collectives: 39.6 us -> none  [local(): total = lax.psum(partial_value, ('box', 'slab'))]
    pallas_call x0 -> x1, Pallas kernels: none -> 32.6 us  [local(): pl.pallas_call(functools.partial(kernel, nbox, nslab, scale), out_shape=(...]
    all_gather x1 -> x0, waiting for transfers between devices: 30.2 us -> none  [local(): whole = lax.all_gather(merged, 'slab', axis=0, tiled=True)]
    ppermute x4 -> x0, waiting for transfers between devices: 11.1 us -> none  [the longest x2 11.1 us: passed_along(): lax.ppermute(value, axis, [(source, source + steps) for source in range(f...]
  transfers between devices with their start and end apart: 5 -> 0, of which waited for: 3 -> 0; matrix products, arithmetic and copies ran while one was open for 9% -> 0% of each run, Pallas kernels for 0% -> 0%
where the time goes in v1:
time: 42.7 us; the launch traced here: 42.4 us
  Pallas kernels  32.6 us (76%)
  local copies, waits for them, and re-layouts  9.15 us (21%)
  between operations  0.66 us (2%)
    pallas_call x1, Pallas kernels, local(): pl.pallas_call(functools.partial(kernel, nbox, nslab, scale), out_shape=(...  32.6 us
    unnamed x20, local copies, waits for them, and re-layouts  9.15 us

profile of v1, /device:TPU:0, one launch (start us, length us, event | category | flops | bytes accessed | tf_op | source)
XLA Modules:
  0.0 42.4 jit_solution(10423977323148038269)
XLA Ops:
  0.6 0.0 copy-start
  0.6 1.6 %copy-done = bf16[1,8,8,128,128]{4,3,2,1,0:T(8,128)(2,1)S(1)} copy-done((bf16[1,8,8,128,128]{4,3,2,1,0:T(8,128)(2,1)S(1)}, bf16[1,8,8,128,128]{4,3,2,1,0:T(8,128)(2,1)}, u32[]{:S(2)}) %copy-start) | copy-done | bytes 2097176
  2.2 0.0 copy-start.1
  2.2 1.0 %copy-done.1 = f32[8,128,128]{2,1,0:T(8,128)S(1)} copy-done((f32[8,128,128]{2,1,0:T(8,128)S(1)}, f32[8,128,128]{2,1,0:T(8,128)}, u32[]{:S(2)}) %copy-start.1) | copy-done | bytes 524312
  3.3 0.0 copy-start.2
  3.3 0.7 %copy-done.2 = bf16[8,27]{1,0:T(8,128)(2,1)S(1)} copy-done((bf16[8,27]{1,0:T(8,128)(2,1)S(1)}, bf16[8,27]{1,0:T(8,128)(2,1)}, u32[]{:S(2)}) %copy-start.2) | copy-done | bytes 456
  3.9 0.0 copy-start.3
  4.0 0.7 %copy-done.3 = s32[8]{0:T(128)S(1)} copy-done((s32[8]{0:T(128)S(1)}, s32[8]{0:T(128)}, u32[]{:S(2)}) %copy-start.3) | copy-done | bytes 56
  4.6 0.0 copy-start.4
  4.6 0.7 %copy-done.4 = s32[8]{0:T(128)S(1)} copy-done((s32[8]{0:T(128)S(1)}, s32[8]{0:T(128)}, u32[]{:S(2)}) %copy-start.4) | copy-done | bytes 56
  5.3 0.0 copy-start.5
  5.3 0.7 %copy-done.5 = s32[8]{0:T(128)S(1)} copy-done((s32[8]{0:T(128)S(1)}, s32[8]{0:T(128)}, u32[]{:S(2)}) %copy-start.5) | copy-done | bytes 56
  5.9 0.0 copy-start.6
  5.9 0.7 %copy-done.6 = s32[8]{0:T(128)S(1)} copy-done((s32[8]{0:T(128)S(1)}, s32[8]{0:T(128)}, u32[]{:S(2)}) %copy-start.6) | copy-done | bytes 56
  6.6 0.0 copy-start.7
  6.6 0.7 %copy-done.7 = s32[8]{0:T(128)S(1)} copy-done((s32[8]{0:T(128)S(1)}, s32[8]{0:T(128)}, u32[]{:S(2)}) %copy-start.7) | copy-done | bytes 56
  7.2 0.0 copy-start.8
  7.2 0.7 %copy-done.8 = s32[8]{0:T(128)S(1)} copy-done((s32[8]{0:T(128)S(1)}, s32[8]{0:T(128)}, u32[]{:S(2)}) %copy-start.8) | copy-done | bytes 56
  7.9 32.6 %shard_map.104 = (bf16[8,8,128,128]{3,2,1,0:T(8,128)(2,1)S(1)}, f32[8,27]{1,0:T(8,128)S(1)}) custom-call(s32[8]{0:T(128)S(1)} %copy-done.3, s32[8]{0:T(128)S(1)} %copy-done.4, s32[8]{0:T(128)S(1)} %copy-done.5, s32[8]{0:T(128)S(1)} %copy-done.6, s32[8]{0:T(128)S(1)} %copy-done.7, s32[8]{0:T(128)S(1)} %copy-done.8, f32[8,128,128]{2,1,0:T(8,128)S(1)} %copy-done.1, ...), custom_call_target="tpu_custom_call" | custom-call | tf_op jit(solution)/shard_map/pallas_call | solution.py:393
  40.5 1.3 %copy.13 = bf16[1,8,8,128,128]{4,3,2,1,0:T(8,128)(2,1)} copy(bf16[1,8,8,128,128]{4,3,2,1,0:T(8,128)(2,1)S(1)} %bitcast.3) | data formatting | bytes 4194304
  41.8 0.6 %copy.14 = f32[8,27]{1,0:T(8,128)} copy(f32[8,27]{1,0:T(8,128)S(1)} %get-tuple-element.9) | data formatting | bytes 1728
Async XLA Ops:
  0.6 1.6 %copy-start = (bf16[1,8,8,128,128]{4,3,2,1,0:T(8,128)(2,1)S(1)}, bf16[1,8,8,128,128]{4,3,2,1,0:T(8,128)(2,1)}, u32[]{:S(2)}) copy-start(bf16[1,8,8,128,128]{4,3,2,1,0:T(8,128)(2,1)} %param.9) | copy-start | bytes 6291460
  2.2 1.0 %copy-start.1 = (f32[8,128,128]{2,1,0:T(8,128)S(1)}, f32[8,128,128]{2,1,0:T(8,128)}, u32[]{:S(2)}) copy-start(f32[8,128,128]{2,1,0:T(8,128)} %cone.1) | copy-start | bytes 1572868
  3.3 0.7 %copy-start.2 = (bf16[8,27]{1,0:T(8,128)(2,1)S(1)}, bf16[8,27]{1,0:T(8,128)(2,1)}, u32[]{:S(2)}) copy-start(bf16[8,27]{1,0:T(8,128)(2,1)} %weight.1) | copy-start | bytes 1300
  3.9 0.7 %copy-start.3 = (s32[8]{0:T(128)S(1)}, s32[8]{0:T(128)}, u32[]{:S(2)}) copy-start(s32[8]{0:T(128)} %bl.1) | copy-start | bytes 100
  4.6 0.7 %copy-start.4 = (s32[8]{0:T(128)S(1)}, s32[8]{0:T(128)}, u32[]{:S(2)}) copy-start(s32[8]{0:T(128)} %bu.1) | copy-start | bytes 100
  5.3 0.7 %copy-start.5 = (s32[8]{0:T(128)S(1)}, s32[8]{0:T(128)}, u32[]{:S(2)}) copy-start(s32[8]{0:T(128)} %plo.1) | copy-start | bytes 100
  5.9 0.7 %copy-start.6 = (s32[8]{0:T(128)S(1)}, s32[8]{0:T(128)}, u32[]{:S(2)}) copy-start(s32[8]{0:T(128)} %pup.1) | copy-start | bytes 100
  6.6 0.7 %copy-start.7 = (s32[8]{0:T(128)S(1)}, s32[8]{0:T(128)}, u32[]{:S(2)}) copy-start(s32[8]{0:T(128)} %wl.1) | copy-start | bytes 100
  7.2 0.7 %copy-start.8 = (s32[8]{0:T(128)S(1)}, s32[8]{0:T(128)}, u32[]{:S(2)}) copy-start(s32[8]{0:T(128)} %wu.1) | copy-start | bytes 100

commit v2 on v1

--- a/solution.py
+++ b/solution.py
@@ -19,6 +19,17 @@
     nbox,
     nslab,
     scale,
+    bl_hbm,
+    bu_hbm,
+    plo_hbm,
+    pup_hbm,
+    wl_hbm,
+    wu_hbm,
+    cone_hbm,
+    weight_hbm,
+    h_hbm,
+    out_hbm,
+    wg,
     bl,
     bu,
     plo,
@@ -27,9 +38,6 @@
     wu,
     cone,
     weight,
-    h_hbm,
-    out_hbm,
-    wg,
     hbuf,
     own,
     z_up,
@@ -50,6 +58,7 @@
     slab_terms,
     msg2,
     box_terms,
+    isem,
     hsem,
     up_s,
     up_r,
@@ -73,6 +82,23 @@
     ch = hbuf.shape[0]
     pairs = ch // 2
 
+    loads = [
+        pltpu.make_async_copy(source, held, isem.at[i])
+        for i, (source, held) in enumerate(
+            (
+                (cone_hbm, cone),
+                (bl_hbm, bl),
+                (bu_hbm, bu),
+                (wl_hbm, wl),
+                (wu_hbm, wu),
+                (plo_hbm, plo),
+                (pup_hbm, pup),
+                (weight_hbm, weight),
+            )
+        )
+    ]
+    for load in loads:
+        load.start()
     h_copy = pltpu.make_async_copy(h_hbm, hbuf, hsem)
     h_copy.start()
 
@@ -88,6 +114,9 @@
 
     lax.fori_loop(1, nslab, greet_slab, 0)
     lax.fori_loop(1, nbox, greet_box, 0)
+
+    for load in loads:
+        load.wait()
 
     def weigh(i, _):
         lower = wl[i].astype(F32) * (1.0 / WDEN)
@@ -386,7 +415,7 @@
     nz = depth * nslab
     scale = 1.0 / math.sqrt(nbox * nz * nx * ny)
     vmem = pl.BlockSpec(memory_space=pltpu.VMEM)
-    smem = pl.BlockSpec(memory_space=pltpu.SMEM)
+    hbm = pl.BlockSpec(memory_space=pltpu.HBM)
     anywhere = pl.BlockSpec(memory_space=pl.ANY)
     dma = pltpu.SemaphoreType.DMA
     link = BF16
@@ -396,9 +425,12 @@
             jax.ShapeDtypeStruct((ch, depth, nx, ny), BF16),
             jax.ShapeDtypeStruct((ch, 27), F32),
         ),
-        in_specs=[smem] * 6 + [vmem, vmem, anywhere],
+        in_specs=[hbm] * 9,
         out_specs=(anywhere, vmem),
         scratch_shapes=[
+            *[pltpu.SMEM((depth,), jnp.int32)] * 6,
+            pltpu.VMEM(cone_grad.shape, F32),
+            pltpu.VMEM(conv_weight.shape, BF16),
             pltpu.VMEM((ch, depth, nx, ny), BF16),
             pltpu.VMEM((nslab, depth, rows, ny), F32),
             pltpu.VMEM((nslab, depth, rows, ny), link),
@@ -419,6 +451,7 @@
             pltpu.VMEM((nslab, 8, 128), F32),
             pltpu.VMEM((8, 128), F32),
             pltpu.VMEM((nbox, 8, 128), F32),
+            dma((8,)),
             dma,
             dma((nslab,)),
             dma((nslab,)),
@@ -435,7 +468,7 @@
             dma((ch // 2,)),
         ],
         compiler_params=pltpu.CompilerParams(
-            collective_id=0, has_side_effects=True, vmem_limit_bytes=44 * 2**20
+            collective_id=0, has_side_effects=True, vmem_limit_bytes=int(62 * 2**20)
         ),
     )(
         box_lower,

time: 42.7 us -> 37.1 us (0.87)
  local copies, waits for them, and re-layouts: 9.15 us -> 3.76 us
    unnamed x20 -> x4, local copies, waits for them, and re-layouts: 9.15 us -> 3.76 us
where the time goes in v2:
time: 37.1 us; the launch traced here: 37 us
  Pallas kernels  32.5 us (88%)
  local copies, waits for them, and re-layouts  3.76 us (10%)
  between operations  0.65 us (2%)
    pallas_call x1, Pallas kernels, local(): pl.pallas_call(functools.partial(kernel, nbox, nslab, scale), out_shape=(...  32.5 us
    unnamed x4, local copies, waits for them, and re-layouts  3.76 us

profile of v2, /device:TPU:0, one launch (start us, length us, event | category | flops | bytes accessed | tf_op | source)
XLA Modules:
  0.0 37.0 jit_solution(4405899334230645487)
XLA Ops:
  0.6 32.5 %shard_map.104 = (bf16[8,8,128,128]{3,2,1,0:T(8,128)(2,1)}, f32[8,27]{1,0:T(8,128)}) custom-call(s32[8]{0:T(128)} %bl_hbm.1, s32[8]{0:T(128)} %bu_hbm.1, s32[8]{0:T(128)} %plo_hbm.1, s32[8]{0:T(128)} %pup_hbm.1, s32[8]{0:T(128)} %wl_hbm.1, s32[8]{0:T(128)} %wu_hbm.1, f32[8,128,128]{2,1,0:T(8,128)} %cone_hbm.1, bf16[8,27]{1,0:T(8,128)(2,1)} %weight_hbm.1, ...), custom_call_target="tpu_custom_call" | custom-call | tf_op jit(solution)/shard_map/pallas_call | solution.py:422
  33.2 0.0 copy-start
  33.2 3.2 %copy.13 = bf16[1,8,8,128,128]{4,3,2,1,0:T(8,128)(2,1)} copy(bf16[1,8,8,128,128]{4,3,2,1,0:T(8,128)(2,1)} %bitcast.3) | data formatting | bytes 4194304
  36.4 0.0 copy-done
  36.4 0.6 %copy.14 = f32[8,27]{1,0:T(8,128)} copy(f32[8,27]{1,0:T(8,128)S(1)} %copy-done) | data formatting | bytes 1728
Async XLA Ops:
  33.2 3.2 %copy-start = (f32[8,27]{1,0:T(8,128)S(1)}, f32[8,27]{1,0:T(8,128)}, u32[]{:S(2)}) copy-start(f32[8,27]{1,0:T(8,128)} %get-tuple-element.9) | copy-start | bytes 2596

commit v3 on v2

--- a/solution.py
+++ b/solution.py
@@ -28,7 +28,7 @@
     cone_hbm,
     weight_hbm,
     h_hbm,
-    out_hbm,
+    out,
     wg,
     bl,
     bu,
@@ -53,7 +53,6 @@
     wide,
     lmat,
     part,
-    obuf,
     msg,
     slab_terms,
     msg2,
@@ -72,7 +71,6 @@
     c_r,
     d_s,
     d_r,
-    osem,
 ):
     g = lax.axis_index("box")
     me = lax.axis_index("slab")
@@ -335,14 +333,10 @@
         d_copy(source, source).wait_recv()
         return 0
 
-    def o_copy(p):
-        return pltpu.make_async_copy(obuf.at[pl.ds(2 * p, 2)], out_hbm.at[pl.ds(2 * p, 2)], osem.at[p])
-
     def pair_grads(p, _):
         grads = jnp.dot(lmat[...], wmat[p], preferred_element_type=F32)
         for cc in range(2):
-            obuf[2 * p + cc] = grads[:, cc * ny : (cc + 1) * ny].reshape(depth, nx, ny).astype(BF16)
-        o_copy(p).start()
+            out[2 * p + cc] = grads[:, cc * ny : (cc + 1) * ny].reshape(depth, nx, ny).astype(BF16)
         return 0
 
     slab_terms[me] = msg[...]
@@ -387,14 +381,9 @@
         d_copy(lax.rem(g + j, nbox), g).wait_send()
         return 0
 
-    def drain_out(p, _):
-        o_copy(p).wait()
-        return 0
-
     lax.fori_loop(0, nslab, drain_z, 0)
     lax.fori_loop(1, nslab, drain_slab, 0)
     lax.fori_loop(1, nbox, drain_box, 0)
-    lax.fori_loop(0, pairs, drain_out, 0)
 
 
 def local(
@@ -416,17 +405,16 @@
     scale = 1.0 / math.sqrt(nbox * nz * nx * ny)
     vmem = pl.BlockSpec(memory_space=pltpu.VMEM)
     hbm = pl.BlockSpec(memory_space=pltpu.HBM)
-    anywhere = pl.BlockSpec(memory_space=pl.ANY)
     dma = pltpu.SemaphoreType.DMA
     link = BF16
     hidden_grad, weight_grad = pl.pallas_call(
         functools.partial(kernel, nbox, nslab, scale),
         out_shape=(
-            jax.ShapeDtypeStruct((ch, depth, nx, ny), BF16),
+            pltpu.VMEM((ch, depth, nx, ny), BF16),
             jax.ShapeDtypeStruct((ch, 27), F32),
         ),
         in_specs=[hbm] * 9,
-        out_specs=(anywhere, vmem),
+        out_specs=(vmem, vmem),
         scratch_shapes=[
             *[pltpu.SMEM((depth,), jnp.int32)] * 6,
             pltpu.VMEM(cone_grad.shape, F32),
@@ -446,7 +434,6 @@
             pltpu.VMEM((27, ch, ny), F32),
             pltpu.VMEM((depth * nx, 9 * ny), BF16),
             pltpu.VMEM((ch // 2, 2 * TAP_ROWS, ny), F32),
-            pltpu.VMEM((ch, depth, nx, ny), BF16),
             pltpu.VMEM((8, 128), F32),
             pltpu.VMEM((nslab, 8, 128), F32),
             pltpu.VMEM((8, 128), F32),
@@ -465,21 +452,25 @@
             dma((nslab,)),
             dma((nbox,)),
             dma((nbox,)),
-            dma((ch // 2,)),
         ],
         compiler_params=pltpu.CompilerParams(
-            collective_id=0, has_side_effects=True, vmem_limit_bytes=int(62 * 2**20)
+            collective_id=0, has_side_effects=True, vmem_limit_bytes=int(44 * 2**20)
         ),
     )(
-        box_lower,
-        box_upper,
-        plane_lower,
-        plane_upper,
-        weight_lower,
-        weight_upper,
-        cone_grad,
-        conv_weight,
-        hidden_field.reshape(ch, depth, nx, ny),
+        *(
+            pltpu.with_memory_space_constraint(x, pltpu.HBM)
+            for x in (
+                box_lower,
+                box_upper,
+                plane_lower,
+                plane_upper,
+                weight_lower,
+                weight_upper,
+                cone_grad,
+                conv_weight,
+                hidden_field.reshape(ch, depth, nx, ny),
+            )
+        )
     )
     return hidden_grad.reshape(hidden_field.shape), weight_grad
 

time: 37.1 us -> 34.6 us (0.933)
  local copies, waits for them, and re-layouts: 3.76 us -> 1.91 us
  Pallas kernels: 32.5 us -> 31.9 us
    unnamed x4 -> x2, local copies, waits for them, and re-layouts: 3.76 us -> 1.91 us
    pallas_call x1, Pallas kernels: 32.5 us -> 31.9 us  [local(): pl.pallas_call(functools.partial(kernel, nbox, nslab, scale), out_shape=(...]
where the time goes in v3:
time: 34.6 us; the launch traced here: 34.5 us
  Pallas kernels  31.9 us (92%)
  local copies, waits for them, and re-layouts  1.91 us (6%)
  between operations  0.64 us (2%)
    pallas_call x1, Pallas kernels, local(): pl.pallas_call(functools.partial(kernel, nbox, nslab, scale), out_shape=(...  31.9 us
    unnamed x2, local copies, waits for them, and re-layouts  1.91 us

profile of v3, /device:TPU:0, one launch (start us, length us, event | category | flops | bytes accessed | tf_op | source)
XLA Modules:
  0.0 34.5 jit_solution(5029127071410872722)
XLA Ops:
  0.6 31.9 %shard_map.104 = (bf16[8,8,128,128]{3,2,1,0:T(8,128)(2,1)S(1)}, f32[8,27]{1,0:T(8,128)S(1)}) custom-call(s32[8]{0:T(128)} %bl_hbm.1, s32[8]{0:T(128)} %bu_hbm.1, s32[8]{0:T(128)} %plo_hbm.1, s32[8]{0:T(128)} %pup_hbm.1, s32[8]{0:T(128)} %wl_hbm.1, s32[8]{0:T(128)} %wu_hbm.1, f32[8,128,128]{2,1,0:T(8,128)} %cone_hbm.1, bf16[8,27]{1,0:T(8,128)(2,1)} %weight_hbm.1, ...), custom_call_target="tpu_custom_call" | custom-call | tf_op jit(solution)/shard_map/pallas_call | solution.py:410
  32.5 1.3 %copy.13 = bf16[1,8,8,128,128]{4,3,2,1,0:T(8,128)(2,1)} copy(bf16[1,8,8,128,128]{4,3,2,1,0:T(8,128)(2,1)S(1)} %bitcast.2) | data formatting | bytes 4194304
  33.9 0.6 %copy.14 = f32[8,27]{1,0:T(8,128)} copy(f32[8,27]{1,0:T(8,128)S(1)} %get-tuple-element.11) | data formatting | bytes 1728
